TPU v7x, 32 devices: a whole 2x2x4 slice. The times are simulated.
32 devices in a mesh: row: 16 (over z, y, core), col: 2 (over x).
Axes of the slice: x: 2, y: 2, z: 4, core: 2. Of those that a mesh axis runs over, the one named last changes fastest.
Arguments:
- left_slots: float32 [16, 1024, 512], P('row', 'col'), may hold values from -0.15625 to 0.15625
- right: float32 [2048, 4096], P('col', 'row'), may hold values from -6 to 6
- previous: float32 [1024, 4096], P('col', 'row'), may hold values from -4 to 4
- offsets: int32 [3], replicated, may hold values from 0 to 3, as said below
- owners: int32 [2, 3], P('col'), may hold values from 0 to 15, as said below
Outputs:
- next_density: float32 [1024, 4096], P('col', 'row')
Inputs may be any that keep to these rules, and one draw needn't show every extreme that they name: `offsets`: distinct, in any order; they include 0 and 3. `owners`: distinct within each grid row.
All inputs are finite; a program needn't handle non-finite values.
Results may differ from a plain program's by a relative error of at most 0.0001.
Values sent between devices are 32-bit elements; how exact they have to be, the bound alone decides.
No kernel may reach another device: no remote copies, remote signals or barrier semaphores. Data moves between devices by JAX's collectives and lax.ppermute only.
A program may use at most 64 MiB of HBM per device.

v0:
```python
import functools

import jax
import jax.numpy as jnp
from jax import lax
from jax.experimental import pallas as pl
from jax.experimental.pallas import tpu as pltpu
from jax.sharding import PartitionSpec as P

PARTS = 2
VMEM = pl.BlockSpec(memory_space=pltpu.VMEM)
SMEM = pl.BlockSpec(memory_space=pltpu.SMEM)
ANY = pl.BlockSpec(memory_space=pl.ANY)


def call(kernel, out_shape, in_specs, operands, flops=0):
    outs = out_shape if isinstance(out_shape, tuple) else (out_shape,)
    moved = sum(x.size * x.dtype.itemsize for x in (*operands, *outs))
    return pl.pallas_call(
        kernel,
        out_shape=out_shape,
        in_specs=in_specs,
        out_specs=jax.tree.map(lambda _: VMEM, out_shape),
        cost_estimate=pl.CostEstimate(flops=flops, bytes_accessed=moved, transcendentals=0),
        compiler_params=pltpu.CompilerParams(vmem_limit_bytes=32 * 1024 * 1024),
    )(*operands)


def split(value):
    high = value.astype(jnp.bfloat16)
    low = (value - high.astype(jnp.float32)).astype(jnp.bfloat16)
    return high, low


def dot(left, right):
    return jnp.dot(left, right, preferred_element_type=jnp.float32)


def flag_kernel(group, few, owners, out):
    count = owners.shape[1]
    upper = jnp.int32(0)
    for number in range(count):
        upper += owners[0, number] // group
    many = jnp.where(jnp.maximum(upper, count - upper) > few, 1, 0)
    out[...] = jnp.full(out.shape, many, jnp.int32)


def copy_kernel(array, wait, out):
    out[...] = array[...]


def pick_kernel(group, owners, arrived, *outs):
    mine, packed, rest = outs[:PARTS], outs[PARTS:-1], outs[-1]
    count, chunk, _ = mine[0].shape
    few = packed[0].shape[0]
    half = lax.axis_index("row") // group
    members = [owners[0, number] % group for number in range(count)]
    slots = [members[0]] * count
    before = jnp.int32(0)
    for number in range(count):
        here = owners[0, number] // group == half
        slots = [jnp.where(here & (before == slot), members[number], old) for slot, old in enumerate(slots)]
        before = jnp.where(here, before + 1, before)
    for part in range(PARTS):
        rows = slice(part * chunk, (part + 1) * chunk)
        for slot in range(count):
            if slot < few:
                packed[part][slot] = arrived[slots[slot], rows, :]
            else:
                rest[part, slot - few] = arrived[slots[slot], rows, :]
            mine[part][slot] = arrived[members[slot], rows, :]


def merge_kernel(group, part, owners, mine, other, rest, *refs):
    out = refs[-1]
    few = other.shape[0]
    half = lax.axis_index("row") // group
    before = jnp.int32(0)
    for number in range(out.shape[0]):
        here = owners[0, number] // group == half

        @pl.when(here)
        def _():
            out[number] = mine[number]

        @pl.when(jnp.logical_not(here) & (before < few))
        def _():
            out[number] = other[jnp.minimum(before, few - 1)]

        @pl.when(jnp.logical_not(here) & (before >= few))
        def _():
            out[number] = rest[part, jnp.maximum(before - few, 0)]

        before = jnp.where(here, before, before + 1)


def right_kernel(offsets, *refs):
    sources, (right_high, right_low) = refs[:-2], refs[-2:]
    count = offsets.shape[0]
    width = right_high.shape[0] // count
    blocks = [ref.at[place:place + width] for ref in sources for place in range(0, ref.shape[0], width)]
    for number in range(count):
        lanes = slice(number * width, (number + 1) * width)
        for block, ref in enumerate(blocks):

            @pl.when(offsets[number] == block)
            def _():
                high, low = split(ref[...])
                right_high[lanes, :] = high
                right_low[lanes, :] = low


def multiply_kernel(part, right_high, right_low, previous, *refs):
    group = len(refs) - part - 3
    pieces, early = refs[:group], refs[group:group + part]
    out, left_high, left_low = refs[group + part:]
    count, chunk, width = pieces[0].shape
    member = lax.axis_index("row") % group
    for number in range(count):
        lanes = slice(number * width, (number + 1) * width)
        for step in range(group):
            place = pl.multiple_of((member ^ step) * chunk, chunk)
            high, low = split(pieces[step][number])
            left_high[pl.ds(place, chunk), lanes] = high
            left_low[pl.ds(place, chunk), lanes] = low
    product = (
        dot(left_high[...], right_low[...])
        + dot(left_low[...], right_high[...])
        + dot(left_high[...], right_high[...])
    )
    if part < PARTS - 1:
        out[...] = product
    else:
        for number, ref in enumerate((*early, product)):
            for place in range(group):
                first = (place * PARTS + number) * chunk
                rows = slice(first, first + chunk)
                out[rows, :] = 2.0 * previous[rows, :] - ref[place * chunk:(place + 1) * chunk, :]


def shards(left_slots, right, previous, offsets, owners):
    own = left_slots[0]
    rows, width = own.shape
    count = offsets.shape[0]
    devices = lax.axis_size("row")
    columns = lax.axis_size("col")
    group = devices // 2
    size = rows // PARTS
    chunk = size // group
    piece = jax.ShapeDtypeStruct((count, chunk, width), own.dtype)

    def swap(array, mask):
        return lax.ppermute(array, "row", [(i, i ^ mask) for i in range(devices)])

    def shift(array, distance):
        pairs = [((i + distance) % columns, i) for i in range(columns)]
        return lax.ppermute(array, "col", pairs)

    groups = [list(range(first, first + group)) for first in range(0, devices, group)]
    arrived = lax.all_to_all(
        own.reshape(group, PARTS * chunk, width), "row", 0, 0, axis_index_groups=groups, tiled=True
    )
    few = (2 * count + 2) // 3
    packed = jax.ShapeDtypeStruct((few, chunk, width), own.dtype)
    extra = jax.ShapeDtypeStruct((PARTS, count - few, chunk, width), own.dtype)
    picked = call(
        functools.partial(pick_kernel, group),
        (piece,) * PARTS + (packed,) * PARTS + (extra,),
        [SMEM, VMEM],
        (owners, arrived),
    )
    mine, sent = picked[:PARTS], picked[PARTS:-1]
    others = [swap(array, group) for array in sent]

    flags = call(
        functools.partial(flag_kernel, group, few),
        jax.ShapeDtypeStruct((8, 128), jnp.int32),
        [SMEM],
        (owners,),
    )
    distance = 1
    while distance < columns:
        flags = flags | shift(flags, distance)
        distance *= 2
    rest = lax.cond(flags[0, 0] == 0, lambda array: array, lambda array: swap(array, group), picked[-1])

    place = right.shape[0] - width
    last, sources = right[place:], [right]
    if place:
        first = jax.ShapeDtypeStruct((place, right.shape[1]), right.dtype)
        first = call(copy_kernel, first, [VMEM, ANY], (right[:place], flags))
    for distance in range(1, columns):
        sources += [shift(first, distance)] if place else []
        sources.append(shift(last, distance))
    terms = jax.ShapeDtypeStruct((count * width, right.shape[1]), jnp.bfloat16)
    right_terms = call(
        right_kernel, (terms, terms), [SMEM] + [VMEM] * len(sources), (offsets, *sources), flops=4 * terms.size
    )

    results = []
    for part in range(PARTS):
        wait = () if part else right_terms[:1]
        merged = call(
            functools.partial(merge_kernel, group, part),
            piece,
            [SMEM, VMEM, VMEM, VMEM] + [ANY] * len(wait),
            (owners, mine[part], others[part], rest, *wait),
        )
        pieces = {0: merged}
        bits = [1 << b for b in range(1, group.bit_length() - 1)]
        for bit in bits if part % 2 else reversed(bits):
            for s in list(pieces):
                pieces[s + bit] = swap(pieces[s], bit)
        for s in list(pieces):
            pieces[s + 1] = swap(pieces[s], 1)
        last = part == PARTS - 1
        operands = (*right_terms, previous, *[pieces[s] for s in range(group)], *results)
        out_shape = jax.ShapeDtypeStruct((rows if last else size, right.shape[1]), previous.dtype)
        moved = sum(x.size * x.dtype.itemsize for x in operands)
        results.append(pl.pallas_call(
            functools.partial(multiply_kernel, part),
            out_shape=out_shape,
            in_specs=[VMEM] * len(operands),
            out_specs=VMEM,
            scratch_shapes=[pltpu.VMEM((size, count * width), jnp.bfloat16)] * 2,
            cost_estimate=pl.CostEstimate(
                flops=6 * size * count * width * right.shape[1], bytes_accessed=moved, transcendentals=0
            ),
            compiler_params=pltpu.CompilerParams(vmem_limit_bytes=32 * 1024 * 1024),
        )(*operands))
    return results[-1]


def solution(mesh):
    return jax.shard_map(
        shards,
        mesh=mesh,
        in_specs=(P("row", "col", None), P("col", "row"), P("col", "row"), P(), P("col", None)),
        out_specs=P("col", "row"),
        check_vma=False,
    )
```

profile of v0, /device:TPU:0, one launch (start us, length us, event | category | flops | bytes accessed | tf_op | source)
XLA Modules:
  0.0 59.6 jit_solution(5927698396359043431)
XLA Ops:
  0.0 0.0 copy-start.8
  0.0 5.4 %all-to-all-start = ((f32[8,64,512]{2,1,0:T(8,128)}), f32[8,64,512]{2,1,0:T(8,128)S(1)}, u32[]{:S(2)}, u32[]{:S(2)}) async-start(f32[8,64,512]{2,1,0:T(8,128)} %bitcast.2), calls=%async_computation | async-start | bytes 2097152 | tf_op jit(solution)/shard_map/all_to_all | solution.py:160
  5.4 0.0 copy-done.8
  5.4 0.6 shard_map.55
  6.0 1.6 %collective-permute-start.1 = (s32[8,128]{1,0:T(8,128)S(1)}, s32[8,128]{1,0:T(8,128)S(1)}, u32[]{:S(2)}, u32[]{:S(2)}) collective-permute-start(s32[8,128]{1,0:T(8,128)S(1)} %shard_map.55), channel_id=1, source_target_pairs={{1,0},{0,1},{3,2},{2,3},{5,4},{4,5},{7,6},{6,7},{9,8},{8,9},{11,10... | collective-permute-start | bytes 12296 | tf_op jit(solution)/shard_map/ppermute | solution.py:157
  7.5 0.0 copy-done
  7.5 0.9 %fusion = (f32[512,256]{1,0:T(8,128)}, f32[512,256]{1,0:T(8,128)S(1)}) fusion(f32[1024,256]{1,0:T(8,128)S(1)} %copy-done), kind=kLoop, calls=%fused_computation | loop fusion | bytes 2097152 | tf_op jit(solution)/shard_map/slice | solution.py:188
  8.4 0.5 collective-permute-start.3
  8.9 0.7 %collective-permute-done.1 = s32[8,128]{1,0:T(8,128)S(1)} collective-permute-done((s32[8,128]{1,0:T(8,128)S(1)}, s32[8,128]{1,0:T(8,128)S(1)}, u32[]{:S(2)}, u32[]{:S(2)}) %collective-permute-start.1) | collective-permute-done | bytes 4128 | tf_op jit(solution)/shard_map/ppermute | solution.py:157
  9.6 0.8 %shard_map.56 = f32[512,256]{1,0:T(8,128)} custom-call(f32[512,256]{1,0:T(8,128)S(1)} %get-tuple-element.25.array, s32[8,128]{1,0:T(8,128)S(1)} %or.3.wait), custom_call_target="tpu_custom_call" | custom-call | bytes 1052672 | tf_op jit(solution)/shard_map/pallas_call | solution.py:19
  10.5 1.5 %collective-permute-start.2 = (f32[512,256]{1,0:T(8,128)}, f32[512,256]{1,0:T(8,128)S(1)}, u32[]{:S(2)}, u32[]{:S(2)}) collective-permute-start(f32[512,256]{1,0:T(8,128)} %shard_map.56), channel_id=1, source_target_pairs={{1,0},{0,1},{3,2},{2,3},{5,4},{4,5},{7,6},{6,7},{9,8},{8,9},{11,10... | collective-permute-start | bytes 1572872 | tf_op jit(solution)/shard_map/ppermute | solution.py:157
  12.0 7.9 %all-to-all-done.arrived = f32[8,64,512]{2,1,0:T(8,128)S(1)} async-done(((f32[8,64,512]{2,1,0:T(8,128)}), f32[8,64,512]{2,1,0:T(8,128)S(1)}, u32[]{:S(2)}, u32[]{:S(2)}) %all-to-all-start) | async-done | bytes 1048608 | tf_op jit(solution)/shard_map/all_to_all | solution.py:160
  19.9 1.3 %shard_map.58 = (f32[3,32,512]{2,1,0:T(8,128)S(1)}, f32[3,32,512]{2,1,0:T(8,128)S(1)}, f32[2,32,512]{2,1,0:T(8,128)}, f32[2,32,512]{2,1,0:T(8,128)S(1)}, f32[2,1,32,512]{3,2,1,0:T(8,128)S(1)}) custom-call(s32[1,3]{1,0:T(1,128)S(1)} %copy-done.8, f32[8,64,512]{2,1,0:T(8,128)S(1)} %all-to-all-done.arrived), custom_call_target="tpu_custom_call" | custom-call | bytes 1835020 | tf_op jit(solution)/shard_map/pallas_call | solution.py:19
  21.1 0.7 %copy-done.4 = f32[3,32,512]{2,1,0:T(8,128)} copy-done((f32[3,32,512]{2,1,0:T(8,128)}, f32[3,32,512]{2,1,0:T(8,128)S(1)}, u32[]{:S(2)}) %copy-start.4) | copy-done | bytes 196632
  21.8 0.7 %copy-done.6 = f32[3,32,512]{2,1,0:T(8,128)} copy-done((f32[3,32,512]{2,1,0:T(8,128)}, f32[3,32,512]{2,1,0:T(8,128)S(1)}, u32[]{:S(2)}) %copy-start.6) | copy-done | bytes 196632
  22.5 2.6 %collective-permute-start.12 = (f32[2,32,512]{2,1,0:T(8,128)}, f32[2,32,512]{2,1,0:T(8,128)S(1)}, u32[]{:S(2)}, u32[]{:S(2)}) collective-permute-start(f32[2,32,512]{2,1,0:T(8,128)} %get-tuple-element.23), channel_id=1, source_target_pairs={{0,16},{2,18},{4,20},{6,22},{8,24},{10,26},{12,28},{14,30},{16,0},... | collective-permute-start | bytes 393224 | tf_op jit(solution)/shard_map/ppermute | solution.py:153
  25.1 0.3 collective-permute-start.4
  25.4 0.5 slice.11
  26.4 0.0 copy-start.9
  26.5 0.0 collective-permute-done.3.refs_2_
  26.5 7.4 %collective-permute-done.2.refs_1_ = f32[512,256]{1,0:T(8,128)S(1)} collective-permute-done((f32[512,256]{1,0:T(8,128)}, f32[512,256]{1,0:T(8,128)S(1)}, u32[]{:S(2)}, u32[]{:S(2)}) %collective-permute-start.2) | collective-permute-done | bytes 524320 | tf_op jit(solution)/shard_map/ppermute | solution.py:157
  33.9 0.8 %copy-done.2 = f32[512,256]{1,0:T(8,128)} copy-done((f32[512,256]{1,0:T(8,128)}, f32[512,256]{1,0:T(8,128)S(1)}, u32[]{:S(2)}) %copy-start.2) | copy-done | bytes 524312
  34.7 0.0 copy-done.9
  34.7 1.0 %copy-done.3 = f32[512,256]{1,0:T(8,128)S(1)} copy-done((f32[512,256]{1,0:T(8,128)S(1)}, f32[512,256]{1,0:T(8,128)}, u32[]{:S(2)}) %copy-start.3) | copy-done | bytes 524312
  35.7 0.9 %shard_map.57 = (bf16[1536,256]{1,0:T(8,128)(2,1)S(1)}, bf16[1536,256]{1,0:T(8,128)(2,1)S(1)}) custom-call(s32[3]{0:T(128)S(1)} %copy-done.9, f32[1024,256]{1,0:T(8,128)S(1)} %copy-done, f32[512,256]{1,0:T(8,128)S(1)} %copy-done.3, f32[512,256]{1,0:T(8,128)S(1)} %collective-permute-done.3.refs_2_), custom_call_target="tpu_custom_call" | custom-call | flops 1572864 | bytes 3670028 | tf_op jit(solution)/shard_map/pallas_call | solution.py:19
  36.6 0.0 copy-start.7
  36.7 0.0 collective-permute-done.12.other
  36.7 0.9 %copy-done.7 = f32[3,32,512]{2,1,0:T(8,128)S(1)} copy-done((f32[3,32,512]{2,1,0:T(8,128)S(1)}, f32[3,32,512]{2,1,0:T(8,128)}, u32[]{:S(2)}) %copy-start.7) | copy-done | bytes 196632
  37.6 0.6 %shard_map.60.refs_0_ = f32[3,32,512]{2,1,0:T(8,128)S(1)} custom-call(s32[1,3]{1,0:T(1,128)S(1)} %copy-done.8, f32[3,32,512]{2,1,0:T(8,128)S(1)} %copy-done.7, f32[2,32,512]{2,1,0:T(8,128)S(1)} %collective-permute-done.12.other, f32[2,1,32,512]{3,2,1,0:T(8,128)S(1)} %get-tuple-element.26.rest, bf16[1536,256]{1,0:T(8,128)(2,1)S(1)} %get-tuple-element.17.refs_0_.right_high), custom_call_target="tpu_custom_call" | custom-call | bytes 1441804 | tf_op jit(solution)/shard_map/pallas_call | solution.py:19
  38.2 0.0 copy-start.1
  38.2 1.7 %collective-permute-start.16 = (f32[3,32,512]{2,1,0:T(8,128)S(1)}, f32[3,32,512]{2,1,0:T(8,128)S(1)}, u32[]{:S(2)}, u32[]{:S(2)}) collective-permute-start(f32[3,32,512]{2,1,0:T(8,128)S(1)} %shard_map.60.refs_0_), channel_id=1, source_target_pairs={{0,8},{2,10},{4,12},{6,14},{8,0},{10,2},{12,4},{14,6},{16,24},{18,... | collective-permute-start | bytes 589832 | tf_op jit(solution)/shard_map/ppermute | solution.py:153
  39.9 1.5 %collective-permute-start.14 = (f32[3,32,512]{2,1,0:T(8,128)S(1)}, f32[3,32,512]{2,1,0:T(8,128)S(1)}, u32[]{:S(2)}, u32[]{:S(2)}) collective-permute-start(f32[3,32,512]{2,1,0:T(8,128)S(1)} %shard_map.60.refs_0_), channel_id=1, source_target_pairs={{0,4},{2,6},{4,0},{6,2},{8,12},{10,14},{12,8},{14,10},{16,20},{18,... | collective-permute-start | bytes 589832 | tf_op jit(solution)/shard_map/ppermute | solution.py:153
  41.4 0.0 collective-permute-start.13
  41.4 0.0 collective-permute-done.4.other
  41.4 0.0 copy-done.5
  41.4 0.6 %shard_map.59.refs_0_ = f32[3,32,512]{2,1,0:T(8,128)S(1)} custom-call(s32[1,3]{1,0:T(1,128)S(1)} %copy-done.8, f32[3,32,512]{2,1,0:T(8,128)S(1)} %copy-done.5, f32[2,32,512]{2,1,0:T(8,128)S(1)} %collective-permute-done.4.other, f32[2,1,32,512]{3,2,1,0:T(8,128)S(1)} %get-tuple-element.26.rest), custom_call_target="tpu_custom_call" | custom-call | bytes 655372 | tf_op jit(solution)/shard_map/pallas_call | solution.py:19
  42.0 0.6 %collective-permute-start.6 = (f32[3,32,512]{2,1,0:T(8,128)S(1)}, f32[3,32,512]{2,1,0:T(8,128)S(1)}, u32[]{:S(2)}, u32[]{:S(2)}) collective-permute-start(f32[3,32,512]{2,1,0:T(8,128)S(1)} %shard_map.59.refs_0_), channel_id=1, source_target_pairs={{0,4},{2,6},{4,0},{6,2},{8,12},{10,14},{12,8},{14,10},{16,20},{18,... | collective-permute-start | bytes 589832 | tf_op jit(solution)/shard_map/ppermute | solution.py:153
  42.6 1.8 %collective-permute-done.16.refs_4_ = f32[3,32,512]{2,1,0:T(8,128)S(1)} collective-permute-done((f32[3,32,512]{2,1,0:T(8,128)S(1)}, f32[3,32,512]{2,1,0:T(8,128)S(1)}, u32[]{:S(2)}, u32[]{:S(2)}) %collective-permute-start.16) | collective-permute-done | bytes 196640 | tf_op jit(solution)/shard_map/ppermute | solution.py:153
  44.5 1.3 %collective-permute-start.18 = (f32[3,32,512]{2,1,0:T(8,128)S(1)}, f32[3,32,512]{2,1,0:T(8,128)S(1)}, u32[]{:S(2)}, u32[]{:S(2)}) collective-permute-start(f32[3,32,512]{2,1,0:T(8,128)S(1)} %collective-permute-done.16.refs_4_), channel_id=1, source_target_pairs={{0,4},{2,6},{4,0},{6,2},{8,12},{10,14},{12,8},{14,10},{16,20},{18,... | collective-permute-start | bytes 589832 | tf_op jit(solution)/shard_map/ppermute | solution.py:153
  45.7 1.5 %collective-permute-start.8 = (f32[3,32,512]{2,1,0:T(8,128)S(1)}, f32[3,32,512]{2,1,0:T(8,128)S(1)}, u32[]{:S(2)}, u32[]{:S(2)}) collective-permute-start(f32[3,32,512]{2,1,0:T(8,128)S(1)} %shard_map.59.refs_0_), channel_id=1, source_target_pairs={{0,8},{2,10},{4,12},{6,14},{8,0},{10,2},{12,4},{14,6},{16,24},{18,... | collective-permute-start | bytes 589832 | tf_op jit(solution)/shard_map/ppermute | solution.py:153
  47.2 0.0 collective-permute-done.14.refs_2_
  47.2 0.0 collective-permute-start.17
  47.2 0.0 collective-permute-done.13.refs_1_
  47.2 0.5 collective-permute-start.15
  47.7 2.4 %collective-permute-done.6.refs_2_ = f32[3,32,512]{2,1,0:T(8,128)S(1)} collective-permute-done((f32[3,32,512]{2,1,0:T(8,128)S(1)}, f32[3,32,512]{2,1,0:T(8,128)S(1)}, u32[]{:S(2)}, u32[]{:S(2)}) %collective-permute-start.6) | collective-permute-done | bytes 196640 | tf_op jit(solution)/shard_map/ppermute | solution.py:153
  50.1 0.8 %collective-permute-start.10 = (f32[3,32,512]{2,1,0:T(8,128)S(1)}, f32[3,32,512]{2,1,0:T(8,128)S(1)}, u32[]{:S(2)}, u32[]{:S(2)}) collective-permute-start(f32[3,32,512]{2,1,0:T(8,128)S(1)} %collective-permute-done.6.refs_2_), channel_id=1, source_target_pairs={{0,8},{2,10},{4,12},{6,14},{8,0},{10,2},{12,4},{14,6},{16,24},{18,... | collective-permute-start | bytes 589832 | tf_op jit(solution)/shard_map/ppermute | solution.py:153
  50.9 3.1 %collective-permute-done.18.refs_6_ = f32[3,32,512]{2,1,0:T(8,128)S(1)} collective-permute-done((f32[3,32,512]{2,1,0:T(8,128)S(1)}, f32[3,32,512]{2,1,0:T(8,128)S(1)}, u32[]{:S(2)}, u32[]{:S(2)}) %collective-permute-start.18) | collective-permute-done | bytes 196640 | tf_op jit(solution)/shard_map/ppermute | solution.py:153
  54.0 0.0 collective-permute-start.19
  54.0 0.0 collective-permute-done.8.refs_4_
  54.0 0.5 collective-permute-start.5
  54.5 0.0 collective-permute-done.17.refs_5_
  54.5 0.1 collective-permute-start.7
  54.6 0.0 collective-permute-done.15.refs_3_
  54.6 0.4 collective-permute-start.9
  55.1 1.3 %collective-permute-done.10.refs_6_ = f32[3,32,512]{2,1,0:T(8,128)S(1)} collective-permute-done((f32[3,32,512]{2,1,0:T(8,128)S(1)}, f32[3,32,512]{2,1,0:T(8,128)S(1)}, u32[]{:S(2)}, u32[]{:S(2)}) %collective-permute-start.10) | collective-permute-done | bytes 196640 | tf_op jit(solution)/shard_map/ppermute | solution.py:153
  56.4 0.0 collective-permute-start.11
  56.4 0.0 collective-permute-done.19.refs_7_
  56.4 0.0 copy-done.1
  56.4 1.0 %shard_map.61.refs_8_ = f32[256,256]{1,0:T(8,128)S(1)} custom-call(bf16[1536,256]{1,0:T(8,128)(2,1)S(1)} %get-tuple-element.17.refs_0_.right_high, bf16[1536,256]{1,0:T(8,128)(2,1)S(1)} %get-tuple-element.18.right_low, f32[512,256]{1,0:T(8,128)S(1)} %copy-done.1, f32[3,32,512]{2,1,0:T(8,128)S(1)} %shard_map.60.refs_0_, ...), custom_call_target="tpu_custom_call" | custom-call | flops 603979776 | bytes 3670016 | tf_op jit(solution)/shard_map/pallas_call | solution.py:220
  57.4 0.0 collective-permute-done.5.refs_1_
  57.4 0.0 collective-permute-done.7.refs_3_
  57.4 0.0 collective-permute-done.9.refs_5_
  57.5 0.4 collective-permute-done.11.refs_7_
  57.8 1.8 %shard_map.62 = f32[512,256]{1,0:T(8,128)} custom-call(bf16[1536,256]{1,0:T(8,128)(2,1)S(1)} %get-tuple-element.17.refs_0_.right_high, bf16[1536,256]{1,0:T(8,128)(2,1)S(1)} %get-tuple-element.18.right_low, f32[512,256]{1,0:T(8,128)S(1)} %copy-done.1, f32[3,32,512]{2,1,0:T(8,128)S(1)} %shard_map.59.refs_0_, ...), custom_call_target="tpu_custom_call" | custom-call | flops 603979776 | bytes 3932160 | tf_op jit(solution)/shard_map/pallas_call | solution.py:220
  (9 shorter events, 0.1 us)
Async XLA Ops:
  0.0 5.4 %copy-start.8 = (s32[1,3]{1,0:T(1,128)S(1)}, s32[1,3]{1,0:T(1,128)}, u32[]{:S(2)}) copy-start(s32[1,3]{1,0:T(1,128)} %owners.7) | copy-start | bytes 40
  0.0 7.5 %copy-start = (f32[1024,256]{1,0:T(8,128)S(1)}, f32[1024,256]{1,0:T(8,128)}, u32[]{:S(2)}) copy-start(f32[1024,256]{1,0:T(8,128)} %refs_0_.1) | copy-start | bytes 3145732
  0.0 19.9 %all-to-all-start = ((f32[8,64,512]{2,1,0:T(8,128)}), f32[8,64,512]{2,1,0:T(8,128)S(1)}, u32[]{:S(2)}, u32[]{:S(2)}) async-start(f32[8,64,512]{2,1,0:T(8,128)} %bitcast.2), calls=%async_computation | async-start | bytes 2097152 | tf_op jit(solution)/shard_map/all_to_all | solution.py:160
  6.0 3.7 %collective-permute-start.1 = (s32[8,128]{1,0:T(8,128)S(1)}, s32[8,128]{1,0:T(8,128)S(1)}, u32[]{:S(2)}, u32[]{:S(2)}) collective-permute-start(s32[8,128]{1,0:T(8,128)S(1)} %shard_map.55), channel_id=1, source_target_pairs={{1,0},{0,1},{3,2},{2,3},{5,4},{4,5},{7,6},{6,7},{9,8},{8,9},{11,10... | collective-permute-start | bytes 12296 | tf_op jit(solution)/shard_map/ppermute | solution.py:157
  8.4 18.1 %collective-permute-start.3 = (f32[512,256]{1,0:T(8,128)}, f32[512,256]{1,0:T(8,128)S(1)}, u32[]{:S(2)}, u32[]{:S(2)}) collective-permute-start(f32[512,256]{1,0:T(8,128)} %get-tuple-element.24), channel_id=1, source_target_pairs={{1,0},{0,1},{3,2},{2,3},{5,4},{4,5},{7,6},{6,7},{9,8},{8,9},{11,10... | collective-permute-start | bytes 1572872 | tf_op jit(solution)/shard_map/ppermute | solution.py:157
  10.5 23.4 %collective-permute-start.2 = (f32[512,256]{1,0:T(8,128)}, f32[512,256]{1,0:T(8,128)S(1)}, u32[]{:S(2)}, u32[]{:S(2)}) collective-permute-start(f32[512,256]{1,0:T(8,128)} %shard_map.56), channel_id=1, source_target_pairs={{1,0},{0,1},{3,2},{2,3},{5,4},{4,5},{7,6},{6,7},{9,8},{8,9},{11,10... | collective-permute-start | bytes 1572872 | tf_op jit(solution)/shard_map/ppermute | solution.py:157
  21.1 0.7 %copy-start.4 = (f32[3,32,512]{2,1,0:T(8,128)}, f32[3,32,512]{2,1,0:T(8,128)S(1)}, u32[]{:S(2)}) copy-start(f32[3,32,512]{2,1,0:T(8,128)S(1)} %get-tuple-element.19.mine) | copy-start | bytes 589828
  21.8 0.7 %copy-start.6 = (f32[3,32,512]{2,1,0:T(8,128)}, f32[3,32,512]{2,1,0:T(8,128)S(1)}, u32[]{:S(2)}) copy-start(f32[3,32,512]{2,1,0:T(8,128)S(1)} %get-tuple-element.22.mine) | copy-start | bytes 589828
  22.5 14.2 %collective-permute-start.12 = (f32[2,32,512]{2,1,0:T(8,128)}, f32[2,32,512]{2,1,0:T(8,128)S(1)}, u32[]{:S(2)}, u32[]{:S(2)}) collective-permute-start(f32[2,32,512]{2,1,0:T(8,128)} %get-tuple-element.23), channel_id=1, source_target_pairs={{0,16},{2,18},{4,20},{6,22},{8,24},{10,26},{12,28},{14,30},{16,0},... | collective-permute-start | bytes 393224 | tf_op jit(solution)/shard_map/ppermute | solution.py:153
  25.1 16.3 %collective-permute-start.4 = (f32[2,32,512]{2,1,0:T(8,128)S(1)}, f32[2,32,512]{2,1,0:T(8,128)S(1)}, u32[]{:S(2)}, u32[]{:S(2)}) collective-permute-start(f32[2,32,512]{2,1,0:T(8,128)S(1)} %get-tuple-element.20), channel_id=1, source_target_pairs={{0,16},{2,18},{4,20},{6,22},{8,24},{10,26},{12,28},{14,30},{16,0},... | collective-permute-start | bytes 393224 | tf_op jit(solution)/shard_map/ppermute | solution.py:153
  26.4 8.2 %copy-start.9 = (s32[3]{0:T(128)S(1)}, s32[3]{0:T(128)}, u32[]{:S(2)}) copy-start(s32[3]{0:T(128)} %offsets.1) | copy-start | bytes 40
  33.9 0.8 %copy-start.2 = (f32[512,256]{1,0:T(8,128)}, f32[512,256]{1,0:T(8,128)S(1)}, u32[]{:S(2)}) copy-start(f32[512,256]{1,0:T(8,128)S(1)} %collective-permute-done.2.refs_1_) | copy-start | bytes 1572868
  34.7 1.0 %copy-start.3 = (f32[512,256]{1,0:T(8,128)S(1)}, f32[512,256]{1,0:T(8,128)}, u32[]{:S(2)}) copy-start(f32[512,256]{1,0:T(8,128)} %copy-done.2) | copy-start | bytes 1572868
  36.6 0.9 %copy-start.7 = (f32[3,32,512]{2,1,0:T(8,128)S(1)}, f32[3,32,512]{2,1,0:T(8,128)}, u32[]{:S(2)}) copy-start(f32[3,32,512]{2,1,0:T(8,128)} %copy-done.6) | copy-start | bytes 589828
  37.6 3.8 %copy-start.5 = (f32[3,32,512]{2,1,0:T(8,128)S(1)}, f32[3,32,512]{2,1,0:T(8,128)}, u32[]{:S(2)}) copy-start(f32[3,32,512]{2,1,0:T(8,128)} %copy-done.4) | copy-start | bytes 589828
  38.2 18.2 %copy-start.1 = (f32[512,256]{1,0:T(8,128)S(1)}, f32[512,256]{1,0:T(8,128)}, u32[]{:S(2)}) copy-start(f32[512,256]{1,0:T(8,128)} %previous.3) | copy-start | bytes 1572868
  38.2 6.3 %collective-permute-start.16 = (f32[3,32,512]{2,1,0:T(8,128)S(1)}, f32[3,32,512]{2,1,0:T(8,128)S(1)}, u32[]{:S(2)}, u32[]{:S(2)}) collective-permute-start(f32[3,32,512]{2,1,0:T(8,128)S(1)} %shard_map.60.refs_0_), channel_id=1, source_target_pairs={{0,8},{2,10},{4,12},{6,14},{8,0},{10,2},{12,4},{14,6},{16,24},{18,... | collective-permute-start | bytes 589832 | tf_op jit(solution)/shard_map/ppermute | solution.py:153
  39.9 7.3 %collective-permute-start.14 = (f32[3,32,512]{2,1,0:T(8,128)S(1)}, f32[3,32,512]{2,1,0:T(8,128)S(1)}, u32[]{:S(2)}, u32[]{:S(2)}) collective-permute-start(f32[3,32,512]{2,1,0:T(8,128)S(1)} %shard_map.60.refs_0_), channel_id=1, source_target_pairs={{0,4},{2,6},{4,0},{6,2},{8,12},{10,14},{12,8},{14,10},{16,20},{18,... | collective-permute-start | bytes 589832 | tf_op jit(solution)/shard_map/ppermute | solution.py:153
  41.4 5.8 %collective-permute-start.13 = (f32[3,32,512]{2,1,0:T(8,128)S(1)}, f32[3,32,512]{2,1,0:T(8,128)S(1)}, u32[]{:S(2)}, u32[]{:S(2)}) collective-permute-start(f32[3,32,512]{2,1,0:T(8,128)S(1)} %shard_map.60.refs_0_), channel_id=1, source_target_pairs={{0,2},{2,0},{4,6},{6,4},{8,10},{10,8},{12,14},{14,12},{16,18},{18,... | collective-permute-start | bytes 589832 | tf_op jit(solution)/shard_map/ppermute | solution.py:153
  42.0 8.1 %collective-permute-start.6 = (f32[3,32,512]{2,1,0:T(8,128)S(1)}, f32[3,32,512]{2,1,0:T(8,128)S(1)}, u32[]{:S(2)}, u32[]{:S(2)}) collective-permute-start(f32[3,32,512]{2,1,0:T(8,128)S(1)} %shard_map.59.refs_0_), channel_id=1, source_target_pairs={{0,4},{2,6},{4,0},{6,2},{8,12},{10,14},{12,8},{14,10},{16,20},{18,... | collective-permute-start | bytes 589832 | tf_op jit(solution)/shard_map/ppermute | solution.py:153
  44.5 9.6 %collective-permute-start.18 = (f32[3,32,512]{2,1,0:T(8,128)S(1)}, f32[3,32,512]{2,1,0:T(8,128)S(1)}, u32[]{:S(2)}, u32[]{:S(2)}) collective-permute-start(f32[3,32,512]{2,1,0:T(8,128)S(1)} %collective-permute-done.16.refs_4_), channel_id=1, source_target_pairs={{0,4},{2,6},{4,0},{6,2},{8,12},{10,14},{12,8},{14,10},{16,20},{18,... | collective-permute-start | bytes 589832 | tf_op jit(solution)/shard_map/ppermute | solution.py:153
  45.7 8.3 %collective-permute-start.8 = (f32[3,32,512]{2,1,0:T(8,128)S(1)}, f32[3,32,512]{2,1,0:T(8,128)S(1)}, u32[]{:S(2)}, u32[]{:S(2)}) collective-permute-start(f32[3,32,512]{2,1,0:T(8,128)S(1)} %shard_map.59.refs_0_), channel_id=1, source_target_pairs={{0,8},{2,10},{4,12},{6,14},{8,0},{10,2},{12,4},{14,6},{16,24},{18,... | collective-permute-start | bytes 589832 | tf_op jit(solution)/shard_map/ppermute | solution.py:153
  47.2 7.3 %collective-permute-start.17 = (f32[3,32,512]{2,1,0:T(8,128)S(1)}, f32[3,32,512]{2,1,0:T(8,128)S(1)}, u32[]{:S(2)}, u32[]{:S(2)}) collective-permute-start(f32[3,32,512]{2,1,0:T(8,128)S(1)} %collective-permute-done.16.refs_4_), channel_id=1, source_target_pairs={{0,2},{2,0},{4,6},{6,4},{8,10},{10,8},{12,14},{14,12},{16,18},{18,... | collective-permute-start | bytes 589832 | tf_op jit(solution)/shard_map/ppermute | solution.py:153
  47.2 7.4 %collective-permute-start.15 = (f32[3,32,512]{2,1,0:T(8,128)S(1)}, f32[3,32,512]{2,1,0:T(8,128)S(1)}, u32[]{:S(2)}, u32[]{:S(2)}) collective-permute-start(f32[3,32,512]{2,1,0:T(8,128)S(1)} %collective-permute-done.14.refs_2_), channel_id=1, source_target_pairs={{0,2},{2,0},{4,6},{6,4},{8,10},{10,8},{12,14},{14,12},{16,18},{18,... | collective-permute-start | bytes 589832 | tf_op jit(solution)/shard_map/ppermute | solution.py:153
  50.1 6.2 %collective-permute-start.10 = (f32[3,32,512]{2,1,0:T(8,128)S(1)}, f32[3,32,512]{2,1,0:T(8,128)S(1)}, u32[]{:S(2)}, u32[]{:S(2)}) collective-permute-start(f32[3,32,512]{2,1,0:T(8,128)S(1)} %collective-permute-done.6.refs_2_), channel_id=1, source_target_pairs={{0,8},{2,10},{4,12},{6,14},{8,0},{10,2},{12,4},{14,6},{16,24},{18,... | collective-permute-start | bytes 589832 | tf_op jit(solution)/shard_map/ppermute | solution.py:153
  54.0 2.4 %collective-permute-start.19 = (f32[3,32,512]{2,1,0:T(8,128)S(1)}, f32[3,32,512]{2,1,0:T(8,128)S(1)}, u32[]{:S(2)}, u32[]{:S(2)}) collective-permute-start(f32[3,32,512]{2,1,0:T(8,128)S(1)} %collective-permute-done.18.refs_6_), channel_id=1, source_target_pairs={{0,2},{2,0},{4,6},{6,4},{8,10},{10,8},{12,14},{14,12},{16,18},{18,... | collective-permute-start | bytes 589832 | tf_op jit(solution)/shard_map/ppermute | solution.py:153
  54.0 3.4 %collective-permute-start.5 = (f32[3,32,512]{2,1,0:T(8,128)S(1)}, f32[3,32,512]{2,1,0:T(8,128)S(1)}, u32[]{:S(2)}, u32[]{:S(2)}) collective-permute-start(f32[3,32,512]{2,1,0:T(8,128)S(1)} %shard_map.59.refs_0_), channel_id=1, source_target_pairs={{0,2},{2,0},{4,6},{6,4},{8,10},{10,8},{12,14},{14,12},{16,18},{18,... | collective-permute-start | bytes 589832 | tf_op jit(solution)/shard_map/ppermute | solution.py:153
  54.5 2.9 %collective-permute-start.7 = (f32[3,32,512]{2,1,0:T(8,128)S(1)}, f32[3,32,512]{2,1,0:T(8,128)S(1)}, u32[]{:S(2)}, u32[]{:S(2)}) collective-permute-start(f32[3,32,512]{2,1,0:T(8,128)S(1)} %collective-permute-done.6.refs_2_), channel_id=1, source_target_pairs={{0,2},{2,0},{4,6},{6,4},{8,10},{10,8},{12,14},{14,12},{16,18},{18,... | collective-permute-start | bytes 589832 | tf_op jit(solution)/shard_map/ppermute | solution.py:153
  54.6 2.8 %collective-permute-start.9 = (f32[3,32,512]{2,1,0:T(8,128)S(1)}, f32[3,32,512]{2,1,0:T(8,128)S(1)}, u32[]{:S(2)}, u32[]{:S(2)}) collective-permute-start(f32[3,32,512]{2,1,0:T(8,128)S(1)} %collective-permute-done.8.refs_4_), channel_id=1, source_target_pairs={{0,2},{2,0},{4,6},{6,4},{8,10},{10,8},{12,14},{14,12},{16,18},{18,... | collective-permute-start | bytes 589832 | tf_op jit(solution)/shard_map/ppermute | solution.py:153
  56.4 1.4 %collective-permute-start.11 = (f32[3,32,512]{2,1,0:T(8,128)S(1)}, f32[3,32,512]{2,1,0:T(8,128)S(1)}, u32[]{:S(2)}, u32[]{:S(2)}) collective-permute-start(f32[3,32,512]{2,1,0:T(8,128)S(1)} %collective-permute-done.10.refs_6_), channel_id=1, source_target_pairs={{0,2},{2,0},{4,6},{6,4},{8,10},{10,8},{12,14},{14,12},{16,18},{18,... | collective-permute-start | bytes 589832 | tf_op jit(solution)/shard_map/ppermute | solution.py:153
where the time goes:
time: 59.9 us; the launch traced here: 59.6 us
  waiting for transfers between devices  25.1 us (42%)
  starting transfers between devices  20.8 us (35%)
  Pallas kernels  7.6 us (13%)
  local copies, waits for them, and re-layouts  5.44 us (9%)
  between operations  0.7 us (1%)
    ppermute x16, starting transfers between devices, swap(): return lax.ppermute(array, 'row', [(i, i ^ mask) for i in range(devices)])  11.8 us
    ppermute x16, waiting for transfers between devices, swap(): return lax.ppermute(array, 'row', [(i, i ^ mask) for i in range(devices)])  9.08 us
    ppermute x3, waiting for transfers between devices, shift(): return lax.ppermute(array, 'col', pairs)  8.14 us
    all_to_all x1, waiting for transfers between devices, shards(): lax.all_to_all(own.reshape(group, PARTS * chunk, width), 'row', 0, 0, axi...  7.9 us
    all_to_all x1, starting transfers between devices, shards(): lax.all_to_all(own.reshape(group, PARTS * chunk, width), 'row', 0, 0, axi...  5.39 us
    pallas_call x6, Pallas kernels, call(): pl.pallas_call(kernel, out_shape=out_shape, in_specs=in_specs, out_specs=...  4.77 us
    unnamed x20, local copies, waits for them, and re-layouts  4.09 us
    ppermute x3, starting transfers between devices, shift(): return lax.ppermute(array, 'col', pairs)  3.58 us
  transfers between devices with their start and end apart: 20, of which 8 were waited for; matrix products, arithmetic and copies ran while one was open for 2% of the time, Pallas kernels for 10%

commit v1 on v0

--- a/solution.py
+++ b/solution.py
@@ -22,7 +22,7 @@
         in_specs=in_specs,
         out_specs=jax.tree.map(lambda _: VMEM, out_shape),
         cost_estimate=pl.CostEstimate(flops=flops, bytes_accessed=moved, transcendentals=0),
-        compiler_params=pltpu.CompilerParams(vmem_limit_bytes=32 * 1024 * 1024),
+        compiler_params=pltpu.CompilerParams(vmem_limit_bytes=16 * 1024 * 1024),
     )(*operands)
 
 
@@ -199,7 +199,7 @@
 
     results = []
     for part in range(PARTS):
-        wait = () if part else right_terms[:1]
+        wait = right_terms[:1] if part == PARTS - 1 else ()
         merged = call(
             functools.partial(merge_kernel, group, part),
             piece,
@@ -226,7 +226,7 @@
             cost_estimate=pl.CostEstimate(
                 flops=6 * size * count * width * right.shape[1], bytes_accessed=moved, transcendentals=0
             ),
-            compiler_params=pltpu.CompilerParams(vmem_limit_bytes=32 * 1024 * 1024),
+            compiler_params=pltpu.CompilerParams(vmem_limit_bytes=16 * 1024 * 1024),
         )(*operands))
     return results[-1]
 

time: 59.9 us -> 55.4 us (0.925)
  local copies, waits for them, and re-layouts: 5.44 us -> 1.39 us
    ppermute x16, waiting for transfers between devices: 9.08 us -> 16.6 us  [swap(): return lax.ppermute(array, 'row', [(i, i ^ mask) for i in range(devices)])]
    ppermute x3, waiting for transfers between devices: 8.14 us -> 0.72 us  [shift(): return lax.ppermute(array, 'col', pairs)]
    unnamed x20 -> x8, local copies, waits for them, and re-layouts: 4.09 us -> 0.01 us
  transfers between devices with their start and end apart: 20 -> 20, of which waited for: 8 -> 8; matrix products, arithmetic and copies ran while one was open for 2% -> 2% of each run, Pallas kernels for 10% -> 11%
where the time goes in v1:
time: 55.4 us; the launch traced here: 55.3 us
  waiting for transfers between devices  25.2 us (45%)
  starting transfers between devices  20.3 us (37%)
  Pallas kernels  7.68 us (14%)
  local copies, waits for them, and re-layouts  1.39 us (3%)
  between operations  0.69 us (1%)
    ppermute x16, waiting for transfers between devices, swap(): return lax.ppermute(array, 'row', [(i, i ^ mask) for i in range(devices)])  16.6 us
    ppermute x16, starting transfers between devices, swap(): return lax.ppermute(array, 'row', [(i, i ^ mask) for i in range(devices)])  11.3 us
    all_to_all x1, waiting for transfers between devices, shards(): lax.all_to_all(own.reshape(group, PARTS * chunk, width), 'row', 0, 0, axi...  7.87 us
    all_to_all x1, starting transfers between devices, shards(): lax.all_to_all(own.reshape(group, PARTS * chunk, width), 'row', 0, 0, axi...  5.39 us
    pallas_call x6, Pallas kernels, call(): pl.pallas_call(kernel, out_shape=out_shape, in_specs=in_specs, out_specs=...  4.87 us
    ppermute x3, starting transfers between devices, shift(): return lax.ppermute(array, 'col', pairs)  3.58 us
    pallas_call x2, Pallas kernels, shards(): pl.pallas_call(functools.partial(multiply_kernel, part), out_shape=out_sh...  2.81 us
  transfers between devices with their start and end apart: 20, of which 8 were waited for; matrix products, arithmetic and copies ran while one was open for 2% of the time, Pallas kernels for 11%

profile of v1, /device:TPU:0, one launch (start us, length us, event | category | flops | bytes accessed | tf_op | source)
XLA Modules:
  0.0 55.3 jit_solution(14577208170999478020)
XLA Ops:
  0.0 0.0 copy-start.2
  0.0 0.0 copy-start
  0.0 5.4 %all-to-all-start = ((f32[8,64,512]{2,1,0:T(8,128)}), f32[8,64,512]{2,1,0:T(8,128)S(1)}, u32[]{:S(2)}, u32[]{:S(2)}) async-start(f32[8,64,512]{2,1,0:T(8,128)} %bitcast.2), calls=%async_computation | async-start | bytes 2097152 | tf_op jit(solution)/shard_map/all_to_all | solution.py:160
  5.4 0.0 copy-done.2
  5.4 0.6 %shard_map.55 = s32[8,128]{1,0:T(8,128)S(1)} custom-call(s32[1,3]{1,0:T(1,128)S(1)} %copy-done.2), custom_call_target="tpu_custom_call" | custom-call | bytes 4108 | tf_op jit(solution)/shard_map/pallas_call | solution.py:19
  6.0 1.6 %collective-permute-start.1 = (s32[8,128]{1,0:T(8,128)S(1)}, s32[8,128]{1,0:T(8,128)S(1)}, u32[]{:S(2)}, u32[]{:S(2)}) collective-permute-start(s32[8,128]{1,0:T(8,128)S(1)} %shard_map.55), channel_id=1, source_target_pairs={{1,0},{0,1},{3,2},{2,3},{5,4},{4,5},{7,6},{6,7},{9,8},{8,9},{11,10... | collective-permute-start | bytes 12296 | tf_op jit(solution)/shard_map/ppermute | solution.py:157
  7.5 0.0 copy-done
  7.5 0.9 %fusion = (f32[512,256]{1,0:T(8,128)}, f32[512,256]{1,0:T(8,128)S(1)}) fusion(f32[1024,256]{1,0:T(8,128)S(1)} %copy-done), kind=kLoop, calls=%fused_computation | loop fusion | bytes 2097152 | tf_op jit(solution)/shard_map/slice | solution.py:188
  8.4 0.5 collective-permute-start.3
  8.9 0.7 %collective-permute-done.1 = s32[8,128]{1,0:T(8,128)S(1)} collective-permute-done((s32[8,128]{1,0:T(8,128)S(1)}, s32[8,128]{1,0:T(8,128)S(1)}, u32[]{:S(2)}, u32[]{:S(2)}) %collective-permute-start.1) | collective-permute-done | bytes 4128 | tf_op jit(solution)/shard_map/ppermute | solution.py:157
  9.6 0.8 %shard_map.56 = f32[512,256]{1,0:T(8,128)} custom-call(f32[512,256]{1,0:T(8,128)S(1)} %get-tuple-element.25.array, s32[8,128]{1,0:T(8,128)S(1)} %or.3.wait), custom_call_target="tpu_custom_call" | custom-call | bytes 1052672 | tf_op jit(solution)/shard_map/pallas_call | solution.py:19
  10.5 1.5 %collective-permute-start.2 = (f32[512,256]{1,0:T(8,128)}, f32[512,256]{1,0:T(8,128)S(1)}, u32[]{:S(2)}, u32[]{:S(2)}) collective-permute-start(f32[512,256]{1,0:T(8,128)} %shard_map.56), channel_id=1, source_target_pairs={{1,0},{0,1},{3,2},{2,3},{5,4},{4,5},{7,6},{6,7},{9,8},{8,9},{11,10... | collective-permute-start | bytes 1572872 | tf_op jit(solution)/shard_map/ppermute | solution.py:157
  12.0 7.9 %all-to-all-done.arrived = f32[8,64,512]{2,1,0:T(8,128)S(1)} async-done(((f32[8,64,512]{2,1,0:T(8,128)}), f32[8,64,512]{2,1,0:T(8,128)S(1)}, u32[]{:S(2)}, u32[]{:S(2)}) %all-to-all-start) | async-done | bytes 1048608 | tf_op jit(solution)/shard_map/all_to_all | solution.py:160
  19.9 1.3 %shard_map.58 = (f32[3,32,512]{2,1,0:T(8,128)S(1)}, f32[3,32,512]{2,1,0:T(8,128)S(1)}, f32[2,32,512]{2,1,0:T(8,128)}, f32[2,32,512]{2,1,0:T(8,128)}, f32[2,1,32,512]{3,2,1,0:T(8,128)S(1)}) custom-call(s32[1,3]{1,0:T(1,128)S(1)} %copy-done.2, f32[8,64,512]{2,1,0:T(8,128)S(1)} %all-to-all-done.arrived), custom_call_target="tpu_custom_call" | custom-call | bytes 1835020 | tf_op jit(solution)/shard_map/pallas_call | solution.py:19
  21.2 2.6 %collective-permute-start.12 = (f32[2,32,512]{2,1,0:T(8,128)}, f32[2,32,512]{2,1,0:T(8,128)S(1)}, u32[]{:S(2)}, u32[]{:S(2)}) collective-permute-start(f32[2,32,512]{2,1,0:T(8,128)} %get-tuple-element.23), channel_id=1, source_target_pairs={{0,16},{2,18},{4,20},{6,22},{8,24},{10,26},{12,28},{14,30},{16,0},... | collective-permute-start | bytes 393224 | tf_op jit(solution)/shard_map/ppermute | solution.py:153
  23.8 0.3 collective-permute-start.4
  24.1 0.5 slice.11
  25.2 8.0 %collective-permute-done.12.other = f32[2,32,512]{2,1,0:T(8,128)S(1)} collective-permute-done((f32[2,32,512]{2,1,0:T(8,128)}, f32[2,32,512]{2,1,0:T(8,128)S(1)}, u32[]{:S(2)}, u32[]{:S(2)}) %collective-permute-start.12) | collective-permute-done | bytes 131104 | tf_op jit(solution)/shard_map/ppermute | solution.py:153
  33.2 0.0 copy-start.3
  33.2 0.6 %shard_map.60.refs_0_ = f32[3,32,512]{2,1,0:T(8,128)S(1)} custom-call(s32[1,3]{1,0:T(1,128)S(1)} %copy-done.2, f32[3,32,512]{2,1,0:T(8,128)S(1)} %get-tuple-element.22.mine, f32[2,32,512]{2,1,0:T(8,128)S(1)} %collective-permute-done.12.other, f32[2,1,32,512]{3,2,1,0:T(8,128)S(1)} %get-tuple-element.26.rest), custom_call_target="tpu_custom_call" | custom-call | bytes 655372 | tf_op jit(solution)/shard_map/pallas_call | solution.py:19
  33.8 0.8 %collective-permute-start.16 = (f32[3,32,512]{2,1,0:T(8,128)S(1)}, f32[3,32,512]{2,1,0:T(8,128)S(1)}, u32[]{:S(2)}, u32[]{:S(2)}) collective-permute-start(f32[3,32,512]{2,1,0:T(8,128)S(1)} %shard_map.60.refs_0_), channel_id=1, source_target_pairs={{0,8},{2,10},{4,12},{6,14},{8,0},{10,2},{12,4},{14,6},{16,24},{18,... | collective-permute-start | bytes 589832 | tf_op jit(solution)/shard_map/ppermute | solution.py:153
  34.6 0.0 collective-permute-done.3.refs_2_
  34.6 0.0 collective-permute-done.2.refs_1_
  34.6 0.0 copy-done.3
  34.6 0.9 %shard_map.57 = (bf16[1536,256]{1,0:T(8,128)(2,1)S(1)}, bf16[1536,256]{1,0:T(8,128)(2,1)S(1)}) custom-call(s32[3]{0:T(128)S(1)} %copy-done.3, f32[1024,256]{1,0:T(8,128)S(1)} %copy-done, f32[512,256]{1,0:T(8,128)S(1)} %collective-permute-done.2.refs_1_, f32[512,256]{1,0:T(8,128)S(1)} %collective-permute-done.3.refs_2_), custom_call_target="tpu_custom_call" | custom-call | flops 1572864 | bytes 3670028 | tf_op jit(solution)/shard_map/pallas_call | solution.py:19
  35.5 1.5 %collective-permute-start.14 = (f32[3,32,512]{2,1,0:T(8,128)S(1)}, f32[3,32,512]{2,1,0:T(8,128)S(1)}, u32[]{:S(2)}, u32[]{:S(2)}) collective-permute-start(f32[3,32,512]{2,1,0:T(8,128)S(1)} %shard_map.60.refs_0_), channel_id=1, source_target_pairs={{0,4},{2,6},{4,0},{6,2},{8,12},{10,14},{12,8},{14,10},{16,20},{18,... | collective-permute-start | bytes 589832 | tf_op jit(solution)/shard_map/ppermute | solution.py:153
  37.0 0.0 collective-permute-start.13
  37.0 0.0 collective-permute-done.4.other
  37.0 0.0 copy-start.1
  37.0 0.6 %shard_map.59.refs_0_ = f32[3,32,512]{2,1,0:T(8,128)S(1)} custom-call(s32[1,3]{1,0:T(1,128)S(1)} %copy-done.2, f32[3,32,512]{2,1,0:T(8,128)S(1)} %get-tuple-element.19.mine, f32[2,32,512]{2,1,0:T(8,128)S(1)} %collective-permute-done.4.other, f32[2,1,32,512]{3,2,1,0:T(8,128)S(1)} %get-tuple-element.26.rest, ...), custom_call_target="tpu_custom_call" | custom-call | bytes 1441804 | tf_op jit(solution)/shard_map/pallas_call | solution.py:19
  37.6 0.6 %collective-permute-start.6 = (f32[3,32,512]{2,1,0:T(8,128)S(1)}, f32[3,32,512]{2,1,0:T(8,128)S(1)}, u32[]{:S(2)}, u32[]{:S(2)}) collective-permute-start(f32[3,32,512]{2,1,0:T(8,128)S(1)} %shard_map.59.refs_0_), channel_id=1, source_target_pairs={{0,4},{2,6},{4,0},{6,2},{8,12},{10,14},{12,8},{14,10},{16,20},{18,... | collective-permute-start | bytes 589832 | tf_op jit(solution)/shard_map/ppermute | solution.py:153
  38.3 2.0 %collective-permute-done.16.refs_4_ = f32[3,32,512]{2,1,0:T(8,128)S(1)} collective-permute-done((f32[3,32,512]{2,1,0:T(8,128)S(1)}, f32[3,32,512]{2,1,0:T(8,128)S(1)}, u32[]{:S(2)}, u32[]{:S(2)}) %collective-permute-start.16) | collective-permute-done | bytes 196640 | tf_op jit(solution)/shard_map/ppermute | solution.py:153
  40.3 1.6 %collective-permute-start.18 = (f32[3,32,512]{2,1,0:T(8,128)S(1)}, f32[3,32,512]{2,1,0:T(8,128)S(1)}, u32[]{:S(2)}, u32[]{:S(2)}) collective-permute-start(f32[3,32,512]{2,1,0:T(8,128)S(1)} %collective-permute-done.16.refs_4_), channel_id=1, source_target_pairs={{0,4},{2,6},{4,0},{6,2},{8,12},{10,14},{12,8},{14,10},{16,20},{18,... | collective-permute-start | bytes 589832 | tf_op jit(solution)/shard_map/ppermute | solution.py:153
  41.9 0.3 collective-permute-start.8
  42.2 0.0 collective-permute-done.14.refs_2_
  42.2 0.0 collective-permute-start.17
  42.2 0.0 collective-permute-done.13.refs_1_
  42.2 0.5 collective-permute-start.15
  42.7 3.5 %collective-permute-done.6.refs_2_ = f32[3,32,512]{2,1,0:T(8,128)S(1)} collective-permute-done((f32[3,32,512]{2,1,0:T(8,128)S(1)}, f32[3,32,512]{2,1,0:T(8,128)S(1)}, u32[]{:S(2)}, u32[]{:S(2)}) %collective-permute-start.6) | collective-permute-done | bytes 196640 | tf_op jit(solution)/shard_map/ppermute | solution.py:153
  46.3 2.0 %collective-permute-start.10 = (f32[3,32,512]{2,1,0:T(8,128)S(1)}, f32[3,32,512]{2,1,0:T(8,128)S(1)}, u32[]{:S(2)}, u32[]{:S(2)}) collective-permute-start(f32[3,32,512]{2,1,0:T(8,128)S(1)} %collective-permute-done.6.refs_2_), channel_id=1, source_target_pairs={{0,8},{2,10},{4,12},{6,14},{8,0},{10,2},{12,4},{14,6},{16,24},{18,... | collective-permute-start | bytes 589832 | tf_op jit(solution)/shard_map/ppermute | solution.py:153
  48.3 1.5 %collective-permute-done.18.refs_6_ = f32[3,32,512]{2,1,0:T(8,128)S(1)} collective-permute-done((f32[3,32,512]{2,1,0:T(8,128)S(1)}, f32[3,32,512]{2,1,0:T(8,128)S(1)}, u32[]{:S(2)}, u32[]{:S(2)}) %collective-permute-start.18) | collective-permute-done | bytes 196640 | tf_op jit(solution)/shard_map/ppermute | solution.py:153
  49.8 0.0 collective-permute-start.19
  49.8 0.0 collective-permute-done.8.refs_4_
  49.8 0.5 collective-permute-start.5
  50.3 0.0 collective-permute-done.17.refs_5_
  50.3 0.1 collective-permute-start.7
  50.4 0.0 collective-permute-done.15.refs_3_
  50.4 0.4 collective-permute-start.9
  50.8 1.2 %collective-permute-done.10.refs_6_ = f32[3,32,512]{2,1,0:T(8,128)S(1)} collective-permute-done((f32[3,32,512]{2,1,0:T(8,128)S(1)}, f32[3,32,512]{2,1,0:T(8,128)S(1)}, u32[]{:S(2)}, u32[]{:S(2)}) %collective-permute-start.10) | collective-permute-done | bytes 196640 | tf_op jit(solution)/shard_map/ppermute | solution.py:153
  52.0 0.0 collective-permute-start.11
  52.0 0.0 collective-permute-done.19.refs_7_
  52.0 0.0 copy-done.1
  52.0 1.0 %shard_map.61.refs_8_ = f32[256,256]{1,0:T(8,128)S(1)} custom-call(bf16[1536,256]{1,0:T(8,128)(2,1)S(1)} %get-tuple-element.17.refs_0_.right_high, bf16[1536,256]{1,0:T(8,128)(2,1)S(1)} %get-tuple-element.18.right_low, f32[512,256]{1,0:T(8,128)S(1)} %copy-done.1, f32[3,32,512]{2,1,0:T(8,128)S(1)} %shard_map.60.refs_0_, ...), custom_call_target="tpu_custom_call" | custom-call | flops 603979776 | bytes 3670016 | tf_op jit(solution)/shard_map/pallas_call | solution.py:220
  53.0 0.0 collective-permute-done.5.refs_1_
  53.0 0.0 collective-permute-done.9.refs_5_
  53.1 0.0 collective-permute-done.7.refs_3_
  53.1 0.4 collective-permute-done.11.refs_7_
  53.4 1.8 %shard_map.62 = f32[512,256]{1,0:T(8,128)} custom-call(bf16[1536,256]{1,0:T(8,128)(2,1)S(1)} %get-tuple-element.17.refs_0_.right_high, bf16[1536,256]{1,0:T(8,128)(2,1)S(1)} %get-tuple-element.18.right_low, f32[512,256]{1,0:T(8,128)S(1)} %copy-done.1, f32[3,32,512]{2,1,0:T(8,128)S(1)} %shard_map.59.refs_0_, ...), custom_call_target="tpu_custom_call" | custom-call | flops 603979776 | bytes 3932160 | tf_op jit(solution)/shard_map/pallas_call | solution.py:220
  (3 shorter events, 0.0 us)
Async XLA Ops:
  0.0 5.4 %copy-start.2 = (s32[1,3]{1,0:T(1,128)S(1)}, s32[1,3]{1,0:T(1,128)}, u32[]{:S(2)}) copy-start(s32[1,3]{1,0:T(1,128)} %owners.7) | copy-start | bytes 40
  0.0 7.5 %copy-start = (f32[1024,256]{1,0:T(8,128)S(1)}, f32[1024,256]{1,0:T(8,128)}, u32[]{:S(2)}) copy-start(f32[1024,256]{1,0:T(8,128)} %refs_0_.1) | copy-start | bytes 3145732
  0.0 19.9 %all-to-all-start = ((f32[8,64,512]{2,1,0:T(8,128)}), f32[8,64,512]{2,1,0:T(8,128)S(1)}, u32[]{:S(2)}, u32[]{:S(2)}) async-start(f32[8,64,512]{2,1,0:T(8,128)} %bitcast.2), calls=%async_computation | async-start | bytes 2097152 | tf_op jit(solution)/shard_map/all_to_all | solution.py:160
  6.0 3.7 %collective-permute-start.1 = (s32[8,128]{1,0:T(8,128)S(1)}, s32[8,128]{1,0:T(8,128)S(1)}, u32[]{:S(2)}, u32[]{:S(2)}) collective-permute-start(s32[8,128]{1,0:T(8,128)S(1)} %shard_map.55), channel_id=1, source_target_pairs={{1,0},{0,1},{3,2},{2,3},{5,4},{4,5},{7,6},{6,7},{9,8},{8,9},{11,10... | collective-permute-start | bytes 12296 | tf_op jit(solution)/shard_map/ppermute | solution.py:157
  8.4 26.2 %collective-permute-start.3 = (f32[512,256]{1,0:T(8,128)}, f32[512,256]{1,0:T(8,128)S(1)}, u32[]{:S(2)}, u32[]{:S(2)}) collective-permute-start(f32[512,256]{1,0:T(8,128)} %get-tuple-element.24), channel_id=1, source_target_pairs={{1,0},{0,1},{3,2},{2,3},{5,4},{4,5},{7,6},{6,7},{9,8},{8,9},{11,10... | collective-permute-start | bytes 1572872 | tf_op jit(solution)/shard_map/ppermute | solution.py:157
  10.5 24.1 %collective-permute-start.2 = (f32[512,256]{1,0:T(8,128)}, f32[512,256]{1,0:T(8,128)S(1)}, u32[]{:S(2)}, u32[]{:S(2)}) collective-permute-start(f32[512,256]{1,0:T(8,128)} %shard_map.56), channel_id=1, source_target_pairs={{1,0},{0,1},{3,2},{2,3},{5,4},{4,5},{7,6},{6,7},{9,8},{8,9},{11,10... | collective-permute-start | bytes 1572872 | tf_op jit(solution)/shard_map/ppermute | solution.py:157
  21.2 12.0 %collective-permute-start.12 = (f32[2,32,512]{2,1,0:T(8,128)}, f32[2,32,512]{2,1,0:T(8,128)S(1)}, u32[]{:S(2)}, u32[]{:S(2)}) collective-permute-start(f32[2,32,512]{2,1,0:T(8,128)} %get-tuple-element.23), channel_id=1, source_target_pairs={{0,16},{2,18},{4,20},{6,22},{8,24},{10,26},{12,28},{14,30},{16,0},... | collective-permute-start | bytes 393224 | tf_op jit(solution)/shard_map/ppermute | solution.py:153
  23.8 13.2 %collective-permute-start.4 = (f32[2,32,512]{2,1,0:T(8,128)}, f32[2,32,512]{2,1,0:T(8,128)S(1)}, u32[]{:S(2)}, u32[]{:S(2)}) collective-permute-start(f32[2,32,512]{2,1,0:T(8,128)} %get-tuple-element.20), channel_id=1, source_target_pairs={{0,16},{2,18},{4,20},{6,22},{8,24},{10,26},{12,28},{14,30},{16,0},... | collective-permute-start | bytes 393224 | tf_op jit(solution)/shard_map/ppermute | solution.py:153
  33.2 1.4 %copy-start.3 = (s32[3]{0:T(128)S(1)}, s32[3]{0:T(128)}, u32[]{:S(2)}) copy-start(s32[3]{0:T(128)} %offsets.1) | copy-start | bytes 40
  33.8 6.5 %collective-permute-start.16 = (f32[3,32,512]{2,1,0:T(8,128)S(1)}, f32[3,32,512]{2,1,0:T(8,128)S(1)}, u32[]{:S(2)}, u32[]{:S(2)}) collective-permute-start(f32[3,32,512]{2,1,0:T(8,128)S(1)} %shard_map.60.refs_0_), channel_id=1, source_target_pairs={{0,8},{2,10},{4,12},{6,14},{8,0},{10,2},{12,4},{14,6},{16,24},{18,... | collective-permute-start | bytes 589832 | tf_op jit(solution)/shard_map/ppermute | solution.py:153
  35.5 6.7 %collective-permute-start.14 = (f32[3,32,512]{2,1,0:T(8,128)S(1)}, f32[3,32,512]{2,1,0:T(8,128)S(1)}, u32[]{:S(2)}, u32[]{:S(2)}) collective-permute-start(f32[3,32,512]{2,1,0:T(8,128)S(1)} %shard_map.60.refs_0_), channel_id=1, source_target_pairs={{0,4},{2,6},{4,0},{6,2},{8,12},{10,14},{12,8},{14,10},{16,20},{18,... | collective-permute-start | bytes 589832 | tf_op jit(solution)/shard_map/ppermute | solution.py:153
  37.0 5.2 %collective-permute-start.13 = (f32[3,32,512]{2,1,0:T(8,128)S(1)}, f32[3,32,512]{2,1,0:T(8,128)S(1)}, u32[]{:S(2)}, u32[]{:S(2)}) collective-permute-start(f32[3,32,512]{2,1,0:T(8,128)S(1)} %shard_map.60.refs_0_), channel_id=1, source_target_pairs={{0,2},{2,0},{4,6},{6,4},{8,10},{10,8},{12,14},{14,12},{16,18},{18,... | collective-permute-start | bytes 589832 | tf_op jit(solution)/shard_map/ppermute | solution.py:153
  37.0 15.0 %copy-start.1 = (f32[512,256]{1,0:T(8,128)S(1)}, f32[512,256]{1,0:T(8,128)}, u32[]{:S(2)}) copy-start(f32[512,256]{1,0:T(8,128)} %previous.3) | copy-start | bytes 1572868
  37.6 8.6 %collective-permute-start.6 = (f32[3,32,512]{2,1,0:T(8,128)S(1)}, f32[3,32,512]{2,1,0:T(8,128)S(1)}, u32[]{:S(2)}, u32[]{:S(2)}) collective-permute-start(f32[3,32,512]{2,1,0:T(8,128)S(1)} %shard_map.59.refs_0_), channel_id=1, source_target_pairs={{0,4},{2,6},{4,0},{6,2},{8,12},{10,14},{12,8},{14,10},{16,20},{18,... | collective-permute-start | bytes 589832 | tf_op jit(solution)/shard_map/ppermute | solution.py:153
  40.3 9.4 %collective-permute-start.18 = (f32[3,32,512]{2,1,0:T(8,128)S(1)}, f32[3,32,512]{2,1,0:T(8,128)S(1)}, u32[]{:S(2)}, u32[]{:S(2)}) collective-permute-start(f32[3,32,512]{2,1,0:T(8,128)S(1)} %collective-permute-done.16.refs_4_), channel_id=1, source_target_pairs={{0,4},{2,6},{4,0},{6,2},{8,12},{10,14},{12,8},{14,10},{16,20},{18,... | collective-permute-start | bytes 589832 | tf_op jit(solution)/shard_map/ppermute | solution.py:153
  41.9 7.9 %collective-permute-start.8 = (f32[3,32,512]{2,1,0:T(8,128)S(1)}, f32[3,32,512]{2,1,0:T(8,128)S(1)}, u32[]{:S(2)}, u32[]{:S(2)}) collective-permute-start(f32[3,32,512]{2,1,0:T(8,128)S(1)} %shard_map.59.refs_0_), channel_id=1, source_target_pairs={{0,8},{2,10},{4,12},{6,14},{8,0},{10,2},{12,4},{14,6},{16,24},{18,... | collective-permute-start | bytes 589832 | tf_op jit(solution)/shard_map/ppermute | solution.py:153
  42.2 8.1 %collective-permute-start.17 = (f32[3,32,512]{2,1,0:T(8,128)S(1)}, f32[3,32,512]{2,1,0:T(8,128)S(1)}, u32[]{:S(2)}, u32[]{:S(2)}) collective-permute-start(f32[3,32,512]{2,1,0:T(8,128)S(1)} %collective-permute-done.16.refs_4_), channel_id=1, source_target_pairs={{0,2},{2,0},{4,6},{6,4},{8,10},{10,8},{12,14},{14,12},{16,18},{18,... | collective-permute-start | bytes 589832 | tf_op jit(solution)/shard_map/ppermute | solution.py:153
  42.2 8.1 %collective-permute-start.15 = (f32[3,32,512]{2,1,0:T(8,128)S(1)}, f32[3,32,512]{2,1,0:T(8,128)S(1)}, u32[]{:S(2)}, u32[]{:S(2)}) collective-permute-start(f32[3,32,512]{2,1,0:T(8,128)S(1)} %collective-permute-done.14.refs_2_), channel_id=1, source_target_pairs={{0,2},{2,0},{4,6},{6,4},{8,10},{10,8},{12,14},{14,12},{16,18},{18,... | collective-permute-start | bytes 589832 | tf_op jit(solution)/shard_map/ppermute | solution.py:153
  46.3 5.7 %collective-permute-start.10 = (f32[3,32,512]{2,1,0:T(8,128)S(1)}, f32[3,32,512]{2,1,0:T(8,128)S(1)}, u32[]{:S(2)}, u32[]{:S(2)}) collective-permute-start(f32[3,32,512]{2,1,0:T(8,128)S(1)} %collective-permute-done.6.refs_2_), channel_id=1, source_target_pairs={{0,8},{2,10},{4,12},{6,14},{8,0},{10,2},{12,4},{14,6},{16,24},{18,... | collective-permute-start | bytes 589832 | tf_op jit(solution)/shard_map/ppermute | solution.py:153
  49.8 2.2 %collective-permute-start.19 = (f32[3,32,512]{2,1,0:T(8,128)S(1)}, f32[3,32,512]{2,1,0:T(8,128)S(1)}, u32[]{:S(2)}, u32[]{:S(2)}) collective-permute-start(f32[3,32,512]{2,1,0:T(8,128)S(1)} %collective-permute-done.18.refs_6_), channel_id=1, source_target_pairs={{0,2},{2,0},{4,6},{6,4},{8,10},{10,8},{12,14},{14,12},{16,18},{18,... | collective-permute-start | bytes 589832 | tf_op jit(solution)/shard_map/ppermute | solution.py:153
  49.8 3.2 %collective-permute-start.5 = (f32[3,32,512]{2,1,0:T(8,128)S(1)}, f32[3,32,512]{2,1,0:T(8,128)S(1)}, u32[]{:S(2)}, u32[]{:S(2)}) collective-permute-start(f32[3,32,512]{2,1,0:T(8,128)S(1)} %shard_map.59.refs_0_), channel_id=1, source_target_pairs={{0,2},{2,0},{4,6},{6,4},{8,10},{10,8},{12,14},{14,12},{16,18},{18,... | collective-permute-start | bytes 589832 | tf_op jit(solution)/shard_map/ppermute | solution.py:153
  50.3 2.8 %collective-permute-start.7 = (f32[3,32,512]{2,1,0:T(8,128)S(1)}, f32[3,32,512]{2,1,0:T(8,128)S(1)}, u32[]{:S(2)}, u32[]{:S(2)}) collective-permute-start(f32[3,32,512]{2,1,0:T(8,128)S(1)} %collective-permute-done.6.refs_2_), channel_id=1, source_target_pairs={{0,2},{2,0},{4,6},{6,4},{8,10},{10,8},{12,14},{14,12},{16,18},{18,... | collective-permute-start | bytes 589832 | tf_op jit(solution)/shard_map/ppermute | solution.py:153
  50.4 2.7 %collective-permute-start.9 = (f32[3,32,512]{2,1,0:T(8,128)S(1)}, f32[3,32,512]{2,1,0:T(8,128)S(1)}, u32[]{:S(2)}, u32[]{:S(2)}) collective-permute-start(f32[3,32,512]{2,1,0:T(8,128)S(1)} %collective-permute-done.8.refs_4_), channel_id=1, source_target_pairs={{0,2},{2,0},{4,6},{6,4},{8,10},{10,8},{12,14},{14,12},{16,18},{18,... | collective-permute-start | bytes 589832 | tf_op jit(solution)/shard_map/ppermute | solution.py:153
  52.0 1.4 %collective-permute-start.11 = (f32[3,32,512]{2,1,0:T(8,128)S(1)}, f32[3,32,512]{2,1,0:T(8,128)S(1)}, u32[]{:S(2)}, u32[]{:S(2)}) collective-permute-start(f32[3,32,512]{2,1,0:T(8,128)S(1)} %collective-permute-done.10.refs_6_), channel_id=1, source_target_pairs={{0,2},{2,0},{4,6},{6,4},{8,10},{10,8},{12,14},{14,12},{16,18},{18,... | collective-permute-start | bytes 589832 | tf_op jit(solution)/shard_map/ppermute | solution.py:153
